TPU v7x, 32 devices: a whole 2x2x4 slice. The times are simulated.
32 devices in a mesh: gx: 4 (over x, core), gy: 8 (over z, y).
Axes of the slice: x: 2, y: 2, z: 4, core: 2. Of those that a mesh axis runs over, the one named last changes fastest.
Arguments:
- hidden: bfloat16 [256, 16384], P('gy'), may hold values from -6 to 6
- norm_gain: bfloat16 [16384], replicated, may hold values from 0.099609375 to 1.8984375
- w_query: bfloat16 [16384, 16384], P('gx', 'gy'), may hold values from -0.046875 to 0.046875
- w_keyval: bfloat16 [16384, 2048], P('gx', 'gy'), may hold values from -0.046875 to 0.046875
- key_cache: bfloat16 [256, 256, 8, 128], P(('gx', 'gy')), may hold values from -1000 to 1000
- value_cache: bfloat16 [256, 256, 8, 128], P(('gx', 'gy')), may hold values from -16 to 16
- lengths: int32 [256], P(('gx', 'gy')), may hold values from 1 to 256, as said below
- w_out: bfloat16 [16384, 16384], P('gy', 'gx'), may hold values from -0.046875 to 0.046875
Outputs:
- mixed: bfloat16 [256, 16384], P('gy', 'gx')
Inputs may be any that keep to these rules, and one draw needn't show every extreme that they name: Slots 0 to lengths - 1 of a row are filled; some row fills all 256.
All inputs are finite; a program needn't handle non-finite values.
Results may differ from a plain program's by a relative error of at most 0.024.
Values may be sent and summed in bfloat16 or wider, within the bound.
A program may use at most 128 MiB of HBM per device.

v0:
```python
import math

import jax
import jax.numpy as jnp
from jax import lax
from jax.sharding import PartitionSpec as P


def rotate_heads(values, position, head_dim):
    half = head_dim // 2
    freq = jnp.exp(-(jnp.arange(half, dtype=jnp.float32) * 2.0 / head_dim) * math.log(500000.0))
    angle = position[:, None] * freq[None, :]
    cosine = jnp.cos(angle)[:, None, :]
    sine = jnp.sin(angle)[:, None, :]
    first = values[..., :half]
    second = values[..., half:]
    return jnp.concatenate(
        [first * cosine - second * sine, second * cosine + first * sine], axis=-1
    )


def attend_rows(query, keyval, key_cache, value_cache, lengths):
    rows, cache_len, kv_heads, head_dim = key_cache.shape
    heads = query.shape[1] // head_dim
    group = heads // kv_heads
    scale = 1.0 / math.sqrt(head_dim)
    position = lengths.astype(jnp.float32)
    rotated = rotate_heads(
        query.astype(jnp.float32).reshape(rows, heads, head_dim), position, head_dim
    ).astype(jnp.bfloat16)
    pairs = keyval.reshape(rows, 2, kv_heads, head_dim)
    new_key = rotate_heads(pairs[:, 0].astype(jnp.float32), position, head_dim).astype(jnp.bfloat16)
    new_value = pairs[:, 1].astype(jnp.float32)
    grouped = rotated.reshape(rows, kv_heads, group, head_dim)
    scores = (
        jnp.einsum("rgqd,rtgd->rgqt", grouped, key_cache, preferred_element_type=jnp.float32)
        * scale
    )
    own = jnp.einsum("rgqd,rgd->rgq", grouped, new_key, preferred_element_type=jnp.float32) * scale
    valid = jnp.arange(cache_len)[None, None, None, :] < lengths[:, None, None, None]
    scores = jnp.where(valid, scores, -jnp.inf)
    top = jnp.maximum(jnp.max(scores, axis=-1), own)
    weights = jnp.exp(scores - top[..., None])
    own_weight = jnp.exp(own - top)
    total = jnp.sum(weights, axis=-1) + own_weight
    probs = (weights / total[..., None]).astype(jnp.bfloat16)
    own_prob = (own_weight / total).astype(jnp.bfloat16)
    result = jnp.einsum("rgqt,rtgd->rgqd", probs, value_cache, preferred_element_type=jnp.float32)
    result = result + own_prob.astype(jnp.float32)[..., None] * new_value[:, :, None, :]
    return result.astype(jnp.bfloat16).reshape(rows, heads * head_dim)


def shards(hidden, norm_gain, w_query, w_keyval, key_cache, value_cache, lengths, w_out):
    width_part = w_query.shape[0]
    query_cols = w_query.shape[1]
    pair_cols = w_keyval.shape[1]
    peers = lax.axis_size("gy")
    values = hidden.astype(jnp.float32)
    inverse = lax.rsqrt(jnp.mean(values * values, axis=1, keepdims=True) + 1e-05)
    normed = (values * inverse * norm_gain.astype(jnp.float32)).astype(jnp.bfloat16)
    own_cols = lax.dynamic_slice_in_dim(normed, lax.axis_index("gx") * width_part, width_part, 1)
    gathered = lax.all_gather(own_cols, "gy", axis=0, tiled=True)
    summed = lax.psum_scatter(
        jnp.concatenate(
            [
                jnp.dot(gathered, w_query, preferred_element_type=jnp.float32),
                jnp.dot(gathered, w_keyval, preferred_element_type=jnp.float32),
            ],
            axis=1,
        ),
        "gx",
        scatter_dimension=0,
        tiled=True,
    )
    packed = summed.astype(jnp.bfloat16)
    local_qkv = lax.all_to_all(packed, "gy", split_axis=0, concat_axis=1, tiled=True)
    rows_dev = local_qkv.shape[0]
    split_cols = local_qkv.reshape(rows_dev, peers, query_cols + pair_cols)
    query = split_cols[:, :, :query_cols].reshape(rows_dev, peers * query_cols)
    keyval = split_cols[:, :, query_cols:].reshape(rows_dev, peers * pair_cols)
    attended = attend_rows(query, keyval, key_cache, value_cache, lengths)
    by_heads = lax.all_to_all(attended, "gy", split_axis=1, concat_axis=0, tiled=True)
    full_rows = lax.all_gather(by_heads, "gx", axis=0, tiled=True)
    partial_out = jnp.dot(full_rows, w_out, preferred_element_type=jnp.float32)
    result = lax.psum_scatter(
        partial_out.astype(jnp.bfloat16), "gy", scatter_dimension=0, tiled=True
    )
    return result


def solution(mesh):
    in_specs = (
        P("gy", None),
        P(),
        P("gx", "gy"),
        P("gx", "gy"),
        P(("gx", "gy"), None, None, None),
        P(("gx", "gy"), None, None, None),
        P(("gx", "gy")),
        P("gy", "gx"),
    )
    out_specs = P("gy", "gx")
    return jax.shard_map(shards, mesh=mesh, in_specs=in_specs, out_specs=out_specs, check_vma=False)
```

profile of v0, /device:TPU:0, one launch (start us, length us, event | category | flops | bytes accessed | tf_op | source)
XLA Modules:
  0.0 246.2 jit_solution(8290286190570894164)
XLA Ops:
  6.6 2.8 %convert_element_type.56 = f32[32,16384]{1,0:T(8,128)} convert(bf16[32,16384]{1,0:T(8,128)(2,1)} %param.8) | non-fusion elementwise | flops 524288 | bytes 3145728 | tf_op jit(solution)/shard_map/convert_element_type | solution.py:58
  9.4 0.3 multiply_reduce_fusion
  9.7 1.9 fusion.18
  11.7 52.1 %all-gather.3.cloned.1.call-done = bf16[256,4096]{1,0:T(8,128)(2,1)} async-done(((bf16[32,4096]{1,0:T(8,128)(2,1)}), bf16[256,4096]{1,0:T(8,128)(2,1)}) %all-gather.3.cloned.1.call-update) | async-done | bytes 2097168 | tf_op jit(solution)/shard_map/all_gather | solution.py:62
  63.8 10.8 %fusion.30 = f32[256,2048]{1,0:T(8,128)S(1)} fusion(bf16[256,4096]{1,0:T(8,128)(2,1)} %all-gather.3.cloned.1.call-done, bf16[4096,2048]{1,0:T(8,128)(2,1)} %param.10), kind=kOutput, calls=%fused_computation.46 | convolution fusion | flops 4294967296 | bytes 20971520 | tf_op jit(solution)/shard_map/dot_general | solution.py:66
  74.6 0.7 fusion.31
  75.3 1.6 pad_maximum_fusion
  76.9 0.6 copy-done.4
  77.6 31.1 %reduce-scatter.3.cloned.1.call-done = f32[64,2304]{1,0:T(8,128)} async-done(((f32[256,2304]{1,0:T(8,128)}), f32[64,2304]{1,0:T(8,128)}) %reduce-scatter.3.cloned.1.call-update) | async-done | bytes 589840 | tf_op jit(solution)/shard_map/reduce_scatter | solution.py:63
  108.6 1.8 convert_bitcast_fusion
  110.4 5.5 %all-to-all-start = ((bf16[8,8,2304]{2,1,0:T(8,128)(2,1)}), bf16[8,8,2304]{2,1,0:T(8,128)(2,1)S(1)}, u32[]{:S(2)}, u32[]{:S(2)}) async-start(bf16[8,8,2304]{2,1,0:T(8,128)(2,1)} %convert_bitcast_fusion), calls=%async_computation.1 | async-start | bytes 589824 | tf_op jit(solution)/shard_map/all_to_all | solution.py:76
  116.2 9.4 %all-to-all-done = bf16[8,8,2304]{2,1,0:T(8,128)(2,1)S(1)} async-done(((bf16[8,8,2304]{2,1,0:T(8,128)(2,1)}), bf16[8,8,2304]{2,1,0:T(8,128)(2,1)S(1)}, u32[]{:S(2)}, u32[]{:S(2)}) %all-to-all-start) | async-done | bytes 294944 | tf_op jit(solution)/shard_map/all_to_all | solution.py:76
  125.7 0.3 copy.18
  126.2 0.2 subtract_convert_fusion
  126.5 0.3 fusion.21
  126.8 3.7 %fusion.29 = (f32[8,8,16]{2,1,0:T(8,128)S(1)}, f32[8,8,16,256]{3,2,1,0:T(8,128)S(1)}) fusion(bf16[8,256,8,128]{3,2,1,0:T(8,128)(2,1)} %param.12, bf16[8,8,16,64]{3,2,1,0:T(8,128)(2,1)S(1)} %bitcast.36, bf16[8,8,16,64]{3,2,1,0:T(8,128)(2,1)S(1)} %bitcast.34, pred[8,256]{1,0:T(8,128)(4,1)S(1)} %iota_compare_fusion), kind=kOutput, calls=%fused_computation.45 | convolution fusion | flops 68418560 | bytes 5511168 | tf_op jit(solution)/shard_map/rgqd,rtgd->rgqt/dot_general | solution.py:36
  130.5 0.4 fusion.16
  130.9 1.0 fusion.13
  132.0 0.1 all_to_all.29
  132.1 0.2 copy.22
  132.2 12.0 %all_to_all.35 = bf16[8,8,2048]{2,0,1:T(8,128)(2,1)} all-to-all(bf16[8,8,2048]{2,0,1:T(8,128)(2,1)S(1)} %copy.22), channel_id=1, replica_groups=mesh['gx'=4,'gy'=8] {'gy'}, dimensions={1} | all-to-all | bytes 524288 | tf_op jit(solution)/shard_map/all_to_all | solution.py:82
  144.3 14.9 %all-gather.5.cloned.1.call-done = bf16[256,2048]{1,0:T(8,128)(2,1)} async-done(((bf16[64,2048]{1,0:T(8,128)(2,1)}), bf16[256,2048]{1,0:T(8,128)(2,1)}) %all-gather.5.cloned.1.call-update) | async-done | bytes 1048592 | tf_op jit(solution)/shard_map/all_gather | solution.py:83
  159.2 11.9 %convolution_convert_fusion = bf16[256,4096]{1,0:T(8,128)(2,1)} fusion(bf16[256,2048]{1,0:T(8,128)(2,1)} %all-gather.5.cloned.1.call-done, bf16[2048,4096]{1,0:T(8,128)(2,1)} %param.15), kind=kOutput, calls=%fused_computation | convolution fusion | flops 4296015872 | bytes 19922944 | tf_op jit(solution)/shard_map/dot_general | solution.py:84
  171.2 68.4 %reduce-scatter.5.cloned.1.call-done = bf16[32,4096]{1,0:T(8,128)(2,1)} async-done(((bf16[256,4096]{1,0:T(8,128)(2,1)}), bf16[32,4096]{1,0:T(8,128)(2,1)}) %reduce-scatter.5.cloned.1.call-update) | async-done | bytes 262160 | tf_op jit(solution)/shard_map/reduce_scatter | solution.py:85
  (35 shorter events, 0.8 us)
Async XLA Ops:
  6.5 68.0 %copy-start = (bf16[4096,256]{1,0:T(8,128)(2,1)S(1)}, bf16[4096,256]{1,0:T(8,128)(2,1)}, u32[]{:S(2)}) copy-start(bf16[4096,256]{1,0:T(8,128)(2,1)} %param.11) | copy-start | bytes 6291460
  6.5 2.9 %copy-start.1 = (bf16[32,16384]{1,0:T(8,128)(2,1)S(1)}, bf16[32,16384]{1,0:T(8,128)(2,1)}, u32[]{:S(2)}) copy-start(bf16[32,16384]{1,0:T(8,128)(2,1)} %param.8) | copy-start | bytes 3145732
  6.5 3.2 %copy-start.3 = (bf16[16384]{0:T(1024)(128)(2,1)S(1)}, bf16[16384]{0:T(1024)(128)(2,1)}, u32[]{:S(2)}) copy-start(bf16[16384]{0:T(1024)(128)(2,1)} %param.9) | copy-start | bytes 98308
  6.5 57.2 %all-gather.3.cloned.1.call-start = ((), (), s32[]{:S(2)}) async-start(), calls=%async_computation.4 | async-start | bytes 2359296 | tf_op jit(solution)/shard_map/all_gather | solution.py:62
  11.6 97.0 %reduce-scatter.3.cloned.1.call-start = ((), (), s32[]{:S(2)}) async-start(), calls=%async_computation.5 | async-start | bytes 2949120 | tf_op jit(solution)/shard_map/reduce_scatter | solution.py:63
  63.8 10.8 %copy-start.2 = (bf16[256,4096]{1,0:T(8,128)(2,1)S(1)}, bf16[256,4096]{1,0:T(8,128)(2,1)}, u32[]{:S(2)}) copy-start(bf16[256,4096]{1,0:T(8,128)(2,1)} %all-gather.3.cloned.1.call-done) | copy-start | bytes 6291460
  76.9 0.7 copy-start.4
  110.4 15.1 %all-to-all-start = ((bf16[8,8,2304]{2,1,0:T(8,128)(2,1)}), bf16[8,8,2304]{2,1,0:T(8,128)(2,1)S(1)}, u32[]{:S(2)}, u32[]{:S(2)}) async-start(bf16[8,8,2304]{2,1,0:T(8,128)(2,1)} %convert_bitcast_fusion), calls=%async_computation.1 | async-start | bytes 589824 | tf_op jit(solution)/shard_map/all_to_all | solution.py:76
  115.9 43.3 %all-gather.5.cloned.1.call-start = ((), (), s32[]{:S(2)}) async-start(), calls=%async_computation.6 | async-start | bytes 1310720 | tf_op jit(solution)/shard_map/all_gather | solution.py:83
  126.8 4.1 %copy-start.5 = (bf16[8,256,8,128]{3,2,1,0:T(8,128)(2,1)S(1)}, bf16[8,256,8,128]{3,2,1,0:T(8,128)(2,1)}, u32[]{:S(2)}) copy-start(bf16[8,256,8,128]{3,2,1,0:T(8,128)(2,1)} %param.13) | copy-start | bytes 12582916
  144.3 95.4 %reduce-scatter.5.cloned.1.call-start = ((), (), s32[]{:S(2)}) async-start(), calls=%async_computation.7 | async-start | bytes 2359296 | tf_op jit(solution)/shard_map/reduce_scatter | solution.py:85
Sparse Core Ops, SparseCore 0:
  11.8 51.9 all-gather.2
  77.0 31.5 reduce-scatter.2
  144.4 14.7 all-gather.4
  171.3 68.2 reduce-scatter.4
where the time goes:
time: 247 us; the launch traced here: 246 us
  waiting for transfers between devices  176 us (71%)
  matrix products  28.4 us (11%)
  between operations  13.3 us (5%)
  blocking collectives  12 us (5%)
  other arithmetic  9.48 us (4%)
  starting transfers between devices  5.63 us (2%)
    reduce_scatter x1, waiting for transfers between devices, shards(): lax.psum_scatter(partial_out.astype(jnp.bfloat16), 'gy', scatter_dimensio...  68.4 us
    all_gather x1, waiting for transfers between devices, shards(): gathered = lax.all_gather(own_cols, 'gy', axis=0, tiled=True)  52.1 us
    reduce_scatter x1, waiting for transfers between devices, shards(): lax.psum_scatter(jnp.concatenate([jnp.dot(gathered, w_query, preferred_el...  31.1 us
    all_gather x1, waiting for transfers between devices, shards(): full_rows = lax.all_gather(by_heads, 'gx', axis=0, tiled=True)  14.9 us
    all_to_all x1, blocking collectives, shards(): lax.all_to_all(attended, 'gy', split_axis=1, concat_axis=0, tiled=True)  12 us
    dot_general x1, matrix products, shards(): partial_out = jnp.dot(full_rows, w_out, preferred_element_type=jnp.float32)  11.9 us
    dot_general x1, matrix products, shards(): jnp.dot(gathered, w_query, preferred_element_type=jnp.float32)  10.8 us
    all_to_all x1, waiting for transfers between devices, shards(): lax.all_to_all(packed, 'gy', split_axis=0, concat_axis=1, tiled=True)  9.38 us
  transfers between devices with their start and end apart: 5, of which 5 were waited for; matrix products, arithmetic and copies ran while one was open for 0% of the time, Pallas kernels for 0%

commit v1 on v0

--- a/solution.py
+++ b/solution.py
@@ -1,9 +1,15 @@
+import functools
 import math
 
 import jax
 import jax.numpy as jnp
 from jax import lax
+from jax.experimental import pallas as pl
+from jax.experimental.pallas import tpu as pltpu
 from jax.sharding import PartitionSpec as P
+
+MESH = pl.DeviceIdType.MESH
+VMEM_BYTES = 56 * 2**20
 
 
 def rotate_heads(values, position, head_dim):
@@ -50,42 +56,469 @@
     return result.astype(jnp.bfloat16).reshape(rows, heads * head_dim)
 
 
+def position_of(index, n):
+    return jnp.where(lax.rem(index, 2) == 0, index // 2, n - (index + 1) // 2)
+
+
+def index_at(position, n):
+    position = lax.rem(position + 2 * n, n)
+    return jnp.where(position < n // 2, 2 * position, 2 * n - 2 * position - 1)
+
+
+def meet(n, gx, me):
+    barrier = pltpu.get_barrier_semaphore()
+    for k in range(1, n):
+        pl.semaphore_signal(
+            barrier, inc=1, device_id=(gx, lax.rem(me + k, n)), device_id_type=MESH
+        )
+    pl.semaphore_signal(barrier, inc=1, device_id=(sibling(gx), me), device_id_type=MESH)
+    pl.semaphore_signal(barrier, inc=1, device_id=(across(gx), me), device_id_type=MESH)
+    pl.semaphore_wait(barrier, n + 1)
+
+
+def sibling(gx):
+    return gx + 1 - 2 * lax.rem(gx, 2)
+
+
+def across(gx):
+    return lax.rem(gx + 2, 4)
+
+
+def send(src, dst, send_sem, recv_sem, device):
+    copy = pltpu.make_async_remote_copy(
+        src_ref=src,
+        dst_ref=dst,
+        send_sem=send_sem,
+        recv_sem=recv_sem,
+        device_id=device,
+        device_id_type=MESH,
+    )
+    return copy
+
+
+def halves_stacked(block):
+    half = block.shape[1] // 2
+    return jnp.concatenate([block[:, :half], block[:, half:]], axis=0)
+
+
+def project_kernel(
+    n, chunks, tiles,
+    hidden_ref, gain_ref, wq_hbm, wkv_hbm, q_out, kv_out,
+    wq, wkv, xg, *rest,
+):
+    count = len(tiles)
+    acc = rest[:count]
+    s1, r1, s2, r2, s3, r3 = (rest[count * (k + 1) : count * (k + 2)] for k in range(6))
+    (w_sem, ag_send, ag_recv, s1_send, s1_recv, s2_send, s2_recv, s3_send, s3_recv) = rest[
+        count * 7 :
+    ]
+    gx = lax.axis_index("gx")
+    me = lax.axis_index("gy")
+    rows = hidden_ref.shape[0]
+    total = rows * n
+    width = chunks * xg.shape[2]
+    piece = xg.shape[2]
+    hops = n // 2
+    loads = []
+    for c in range(chunks):
+        loads.append(
+            (
+                pltpu.make_async_copy(
+                    wq_hbm.at[pl.ds(c * piece, piece), :], wq.at[c], w_sem.at[0, c]
+                ),
+                pltpu.make_async_copy(
+                    wkv_hbm.at[pl.ds(c * piece, piece), :], wkv.at[c], w_sem.at[1, c]
+                ),
+            )
+        )
+    for pair in loads:
+        pair[0].start()
+        pair[1].start()
+
+    squares = jnp.zeros((rows, 128), jnp.float32)
+    features = hidden_ref.shape[1]
+    for k in range(0, features, 1024):
+        block = hidden_ref[:, k : k + 1024].astype(jnp.float32)
+        block = block * block
+        for part in range(0, 1024, 128):
+            squares = squares + block[:, part : part + 128]
+    mean = jnp.sum(squares, axis=1, keepdims=True) * (1.0 / features)
+    inverse = lax.rsqrt(mean + 1e-05)
+
+    place = position_of(me, n)
+    ahead = index_at(place + 1, n)
+    behind = index_at(place - 1, n)
+    targets = (ahead, behind)
+
+    def slot(owner, c):
+        return xg.at[c, pl.ds(pl.multiple_of(owner * rows, rows), rows), :]
+
+    def used(d, c, s):
+        return s < hops - 1 or c % 2 == d
+
+    def ring(d, c, s):
+        owner = index_at(place - s if d == 0 else place + s, n)
+        ref = slot(owner, c)
+        return send(ref, ref, ag_send.at[d, c, s], ag_recv.at[d, c, s], (gx, targets[d]))
+
+    def ring_in(d, c, s):
+        owner = index_at(place - s - 1 if d == 0 else place + s + 1, n)
+        ref = slot(owner, c)
+        return send(ref, ref, ag_send.at[d, c, s], ag_recv.at[d, c, s], (gx, targets[d]))
+
+    for c in range(chunks):
+        offset = pl.multiple_of(gx * width + c * piece, piece)
+        block = hidden_ref[:, pl.ds(offset, piece)].astype(jnp.float32)
+        gain = gain_ref[:, pl.ds(offset, piece)].astype(jnp.float32)
+        xg[c, pl.ds(pl.multiple_of(me * rows, rows), rows), :] = (
+            block * inverse * gain
+        ).astype(jnp.bfloat16)
+    meet(n, gx, me)
+
+    started = []
+
+    def go(copy):
+        copy.start()
+        started.append(copy)
+
+    def add_product(t, c):
+        source, start, wide = tiles[t]
+        weights = wq if source == 0 else wkv
+        step = min(512, wide)
+
+        def body(k, carry):
+            at = pl.multiple_of(k * step, step) if wide > step else 0
+            product = jnp.dot(
+                xg[c],
+                weights[c, :, pl.ds(start + at, step)],
+                preferred_element_type=jnp.float32,
+            )
+            if c == 0:
+                acc[t][:, pl.ds(at, step)] = product
+            else:
+                acc[t][:, pl.ds(at, step)] += product
+            return carry
+
+        if wide > step:
+            lax.fori_loop(0, wide // step, body, 0)
+        else:
+            body(0, 0)
+
+    part_rows = total // 4
+    core = lax.rem(gx, 2)
+    xi = gx // 2
+
+    def part(gxi):
+        return pl.ds(pl.multiple_of(gxi * part_rows, part_rows), part_rows)
+
+    first = []
+    for time in range(chunks + hops):
+        if time == 0:
+            for c in range(min(2, chunks)):
+                for d in (0, 1):
+                    if used(d, c, 0):
+                        go(ring(d, c, 0))
+        elif time + 1 < chunks:
+            for d in (0, 1):
+                if used(d, time + 1, 0):
+                    go(ring(d, time + 1, 0))
+        for c in range(chunks):
+            s = time - c
+            if 1 <= s < hops:
+                for d in (0, 1):
+                    if used(d, c, s - 1):
+                        ring_in(d, c, s - 1).wait_recv()
+                    if used(d, c, s):
+                        go(ring(d, c, s))
+        c = time - hops
+        if 0 <= c < chunks:
+            for d in (0, 1):
+                if used(d, c, hops - 1):
+                    ring_in(d, c, hops - 1).wait_recv()
+            loads[c][0].wait()
+            loads[c][1].wait()
+            for t in range(count):
+                add_product(t, c)
+                if c == chunks - 1:
+                    for x in (0, 1):
+                        s1[t][x] = acc[t][part(2 * x + 1 - core), :].astype(jnp.bfloat16)
+                    copy = send(s1[t], r1[t], s1_send.at[t], s1_recv.at[t], (sibling(gx), me))
+                    go(copy)
+                    first.append(copy)
+    second = []
+    for t in range(count):
+        first[t].wait_recv()
+        s2[t][...] = (
+            acc[t][part(across(gx)), :] + r1[t][1 - xi].astype(jnp.float32)
+        ).astype(jnp.bfloat16)
+        copy = send(s2[t], r2[t], s2_send.at[t], s2_recv.at[t], (across(gx), me))
+        go(copy)
+        second.append(copy)
+    for t in range(count):
+        second[t].wait_recv()
+        block = acc[t][part(gx), :] + r1[t][xi].astype(jnp.float32) + r2[t][...].astype(jnp.float32)
+        for p in range(n):
+            s3[t][p] = halves_stacked(block[8 * p : 8 * p + 8, :]).astype(jnp.bfloat16)
+        for k in range(1, n):
+            go(
+                send(
+                    s3[t].at[lax.rem(me + k, n)],
+                    r3[t].at[me],
+                    s3_send.at[t, k],
+                    s3_recv.at[t, k],
+                    (gx, lax.rem(me + k, n)),
+                )
+            )
+        r3[t][me] = s3[t][me]
+    for t in range(count):
+        for k in range(1, n):
+            owner = lax.rem(me + n - k, n)
+            send(
+                s3[t].at[owner], r3[t].at[owner], s3_send.at[t, k], s3_recv.at[t, k], (gx, owner)
+            ).wait_recv()
+        source, start, wide = tiles[t]
+        out = q_out if source == 0 else kv_out
+        columns = out.shape[1] // n
+        half = wide // 2
+        for p in range(n):
+            block = r3[t][p].astype(jnp.float32)
+            at = p * columns + start
+            out[:, at : at + half] = block[:8].astype(jnp.bfloat16)
+            out[:, at + half : at + wide] = block[8:].astype(jnp.bfloat16)
+    for copy in started:
+        copy.wait_send()
+
+
+def project(hidden, gain, w_query, w_keyval, n):
+    rows, features = hidden.shape
+    width, q_cols = w_query.shape
+    kv_cols = w_keyval.shape[1]
+    chunks = 4
+    piece = width // chunks
+    total = rows * n
+    step = min(1024, q_cols)
+    tiles = [(0, k, step) for k in range(0, q_cols, step)] + [(1, 0, kv_cols)]
+    count = len(tiles)
+    hops = n // 2
+    bf = jnp.bfloat16
+    scratch = [
+        pltpu.VMEM((chunks, piece, q_cols), bf),
+        pltpu.VMEM((chunks, piece, kv_cols), bf),
+        pltpu.VMEM((chunks, total, piece), bf),
+    ]
+    scratch += [pltpu.VMEM((total, w), jnp.float32) for _, _, w in tiles]
+    for shape in (
+        lambda w: (2, total // 4, w),
+        lambda w: (2, total // 4, w),
+        lambda w: (total // 4, w),
+        lambda w: (total // 4, w),
+        lambda w: (n, 16, w // 2),
+        lambda w: (n, 16, w // 2),
+    ):
+        scratch += [pltpu.VMEM(shape(w), bf) for _, _, w in tiles]
+    dma = pltpu.SemaphoreType.DMA
+    scratch += [
+        dma((2, chunks)),
+        dma((2, chunks, hops)), dma((2, chunks, hops)),
+        dma((count,)), dma((count,)),
+        dma((count,)), dma((count,)),
+        dma((count, n)), dma((count, n)),
+    ]
+    vmem = pl.BlockSpec(memory_space=pltpu.VMEM)
+    hbm = pl.BlockSpec(memory_space=pl.ANY)
+    return pl.pallas_call(
+        functools.partial(project_kernel, n, chunks, tiles),
+        out_shape=[
+            jax.ShapeDtypeStruct((8, n * q_cols), bf),
+            jax.ShapeDtypeStruct((8, n * kv_cols), bf),
+        ],
+        in_specs=[vmem, vmem, hbm, hbm],
+        out_specs=[vmem, vmem],
+        scratch_shapes=scratch,
+        compiler_params=pltpu.CompilerParams(
+            collective_id=0, has_side_effects=True, vmem_limit_bytes=VMEM_BYTES
+        ),
+        cost_estimate=pl.CostEstimate(
+            flops=2 * total * width * (q_cols + kv_cols),
+            bytes_accessed=2 * width * (q_cols + kv_cols),
+            transcendentals=0,
+        ),
+        name="project",
+    )(hidden, gain, w_query, w_keyval)
+
+
+def combine_kernel(
+    n, chunks,
+    att_ref, w_hbm, out_ref,
+    w, packed, xa, xs, part, first, ringbuf,
+    w_sem, a_send, a_recv, x_send, x_recv, c_send, c_recv, e_send, e_recv, g_send, g_recv,
+):
+    gx = lax.axis_index("gx")
+    me = lax.axis_index("gy")
+    columns = w.shape[1]
+    piece = w.shape[2]
+    half = columns // 2
+    hops = n // 2
+    total = xs.shape[0]
+    rows = total // n
+    loads = [
+        pltpu.make_async_copy(w_hbm.at[:, pl.ds(c * piece, piece)], w.at[c], w_sem.at[c])
+        for c in range(chunks)
+    ]
+    for p in range(n):
+        block = att_ref[:, p * columns : (p + 1) * columns].astype(jnp.float32)
+        packed[p] = halves_stacked(block).astype(jnp.bfloat16)
+    started = []
+
+    def go(copy):
+        copy.start()
+        started.append(copy)
+
+    meet(n, gx, me)
+    for k in range(1, n):
+        to = lax.rem(me + k, n)
+        go(send(packed.at[to], xa.at[gx, me], a_send.at[k], a_recv.at[k], (gx, to)))
+    for load in loads:
+        load.start()
+    xa[gx, me] = packed[me]
+    other = across(gx)
+    twin = sibling(gx)
+    far = across(twin)
+    for k in range(n):
+        owner = lax.rem(me + n - k, n)
+        if k:
+            send(packed.at[owner], xa.at[gx, owner], a_send.at[k], a_recv.at[k], (gx, owner)).wait_recv()
+        ref = xa.at[gx, owner]
+        go(send(ref, ref, x_send.at[k], x_recv.at[k], (other, me)))
+        go(send(ref, ref, c_send.at[k], c_recv.at[k], (twin, me)))
+    for k in range(n):
+        owner = lax.rem(me + n - k, n)
+        ref = xa.at[other, owner]
+        send(ref, ref, x_send.at[k], x_recv.at[k], (other, me)).wait_recv()
+        go(send(ref, ref, e_send.at[k], e_recv.at[k], (twin, me)))
+    for k in range(n):
+        owner = lax.rem(me + n - k, n)
+        ref = xa.at[twin, owner]
+        send(ref, ref, c_send.at[k], c_recv.at[k], (twin, me)).wait_recv()
+    for k in range(n):
+        owner = lax.rem(me + n - k, n)
+        ref = xa.at[far, owner]
+        send(ref, ref, e_send.at[k], e_recv.at[k], (twin, me)).wait_recv()
+    for i in range(4):
+        for p in range(0, n, 2):
+            low = xa[i, p].astype(jnp.float32)
+            high = xa[i, p + 1].astype(jnp.float32)
+            at = (i * n + p) * 8
+            xs[at : at + 16, :half] = jnp.concatenate([low[:8], high[:8]], axis=0).astype(jnp.bfloat16)
+            xs[at : at + 16, half:] = jnp.concatenate([low[8:], high[8:]], axis=0).astype(jnp.bfloat16)
+
+    place = position_of(me, n)
+    targets = (index_at(place + 1, n), index_at(place - 1, n))
+
+    def used(d, c, s):
+        return s > 0 or c % 2 == d
+
+    def own(c, owner):
+        return part[c, pl.ds(pl.multiple_of(owner * rows, rows), rows), :]
+
+    def hop(d, c, s):
+        begins = not (s > 0 and used(d, c, s - 1))
+        src = first.at[d, c] if begins else ringbuf.at[d, c, s - 1]
+        return send(src, ringbuf.at[d, c, s], g_send.at[d, c, s], g_recv.at[d, c, s], (gx, targets[d]))
+
+    def pass_on(d, c, s):
+        away = hops - s
+        owner = index_at(place + away if d == 0 else place - away, n)
+        value = own(c, owner)
+        if s > 0 and used(d, c, s - 1):
+            hop(d, c, s - 1).wait_recv()
+            ringbuf[d, c, s - 1] = (
+                value + ringbuf[d, c, s - 1].astype(jnp.float32)
+            ).astype(jnp.bfloat16)
+        else:
+            first[d, c] = value.astype(jnp.bfloat16)
+        go(hop(d, c, s))
+
+    step = min(512, piece)
+    for time in range(chunks + hops):
+        for c in range(chunks):
+            s = time - c
+            if 1 <= s < hops:
+                for d in (0, 1):
+                    pass_on(d, c, s)
+            if s == hops:
+                value = own(c, me)
+                for d in (0, 1):
+                    hop(d, c, hops - 1).wait_recv()
+                    value = value + ringbuf[d, c, hops - 1].astype(jnp.float32)
+                out_ref[:, c * piece : (c + 1) * piece] = value.astype(jnp.bfloat16)
+        if time < chunks:
+            c = time
+            loads[c].wait()
+
+            def body(k, carry):
+                at = pl.multiple_of(k * step, step)
+                part[c, :, pl.ds(at, step)] = jnp.dot(
+                    xs[...], w[c, :, pl.ds(at, step)], preferred_element_type=jnp.float32
+                )
+                return carry
+
+            lax.fori_loop(0, piece // step, body, 0)
+            for d in (0, 1):
+                if used(d, c, 0):
+                    pass_on(d, c, 0)
+    for copy in started:
+        copy.wait_send()
+
+
+def combine(attended, w_out, n):
+    columns, width = w_out.shape
+    chunks = 4
+    piece = width // chunks
+    total = 4 * n * 8
+    rows = total // n
+    hops = n // 2
+    bf = jnp.bfloat16
+    dma = pltpu.SemaphoreType.DMA
+    vmem = pl.BlockSpec(memory_space=pltpu.VMEM)
+    hbm = pl.BlockSpec(memory_space=pl.ANY)
+    return pl.pallas_call(
+        functools.partial(combine_kernel, n, chunks),
+        out_shape=jax.ShapeDtypeStruct((rows, width), bf),
+        in_specs=[vmem, hbm],
+        out_specs=vmem,
+        scratch_shapes=[
+            pltpu.VMEM((chunks, columns, piece), bf),
+            pltpu.VMEM((n, 16, columns // 2), bf),
+            pltpu.VMEM((4, n, 16, columns // 2), bf),
+            pltpu.VMEM((total, columns), bf),
+            pltpu.VMEM((chunks, total, piece), jnp.float32),
+            pltpu.VMEM((2, chunks, rows, piece), bf),
+            pltpu.VMEM((2, chunks, hops, rows, piece), bf),
+            dma((chunks,)),
+            dma((n,)), dma((n,)),
+            dma((n,)), dma((n,)),
+            dma((n,)), dma((n,)),
+            dma((n,)), dma((n,)),
+            dma((2, chunks, hops)), dma((2, chunks, hops)),
+        ],
+        compiler_params=pltpu.CompilerParams(
+            collective_id=1, has_side_effects=True, vmem_limit_bytes=VMEM_BYTES
+        ),
+        cost_estimate=pl.CostEstimate(
+            flops=2 * total * columns * width,
+            bytes_accessed=2 * columns * width,
+            transcendentals=0,
+        ),
+        name="combine",
+    )(attended, w_out)
+
+
 def shards(hidden, norm_gain, w_query, w_keyval, key_cache, value_cache, lengths, w_out):
-    width_part = w_query.shape[0]
-    query_cols = w_query.shape[1]
-    pair_cols = w_keyval.shape[1]
     peers = lax.axis_size("gy")
-    values = hidden.astype(jnp.float32)
-    inverse = lax.rsqrt(jnp.mean(values * values, axis=1, keepdims=True) + 1e-05)
-    normed = (values * inverse * norm_gain.astype(jnp.float32)).astype(jnp.bfloat16)
-    own_cols = lax.dynamic_slice_in_dim(normed, lax.axis_index("gx") * width_part, width_part, 1)
-    gathered = lax.all_gather(own_cols, "gy", axis=0, tiled=True)
-    summed = lax.psum_scatter(
-        jnp.concatenate(
-            [
-                jnp.dot(gathered, w_query, preferred_element_type=jnp.float32),
-                jnp.dot(gathered, w_keyval, preferred_element_type=jnp.float32),
-            ],
-            axis=1,
-        ),
-        "gx",
-        scatter_dimension=0,
-        tiled=True,
-    )
-    packed = summed.astype(jnp.bfloat16)
-    local_qkv = lax.all_to_all(packed, "gy", split_axis=0, concat_axis=1, tiled=True)
-    rows_dev = local_qkv.shape[0]
-    split_cols = local_qkv.reshape(rows_dev, peers, query_cols + pair_cols)
-    query = split_cols[:, :, :query_cols].reshape(rows_dev, peers * query_cols)
-    keyval = split_cols[:, :, query_cols:].reshape(rows_dev, peers * pair_cols)
+    query, keyval = project(hidden, norm_gain.reshape(1, -1), w_query, w_keyval, peers)
     attended = attend_rows(query, keyval, key_cache, value_cache, lengths)
-    by_heads = lax.all_to_all(attended, "gy", split_axis=1, concat_axis=0, tiled=True)
-    full_rows = lax.all_gather(by_heads, "gx", axis=0, tiled=True)
-    partial_out = jnp.dot(full_rows, w_out, preferred_element_type=jnp.float32)
-    result = lax.psum_scatter(
-        partial_out.astype(jnp.bfloat16), "gy", scatter_dimension=0, tiled=True
-    )
-    return result
+    return combine(attended, w_out, peers)
 
 
 def solution(mesh):

time: 247 us -> 114 us (0.46)
  waiting for transfers between devices: 176 us -> 0 us
  Pallas kernels: 0 us -> 103 us
  matrix products: 28.4 us -> 2.64 us
  between operations: 13.3 us -> 0.12 us
  blocking collectives: 12 us -> 0 us
  starting transfers between devices: 5.63 us -> 0 us
  other arithmetic: 9.48 us -> 4.41 us
  local copies, waits for them, and re-layouts: 1.36 us -> 4.09 us
    pallas_call x0 -> x2, Pallas kernels: none -> 103 us  [the longest x1 54.7 us: project(): pl.pallas_call(functools.partial(project_kernel, n, chunks, tiles), out_s...]
    reduce_scatter x2 -> x0, waiting for transfers between devices: 99.5 us -> none  [the longest x1 68.4 us: shards(): lax.psum_scatter(partial_out.astype(jnp.bfloat16), 'gy', scatter_dimensio...]
    all_gather x2 -> x0, waiting for transfers between devices: 67 us -> none  [the longest x1 52.1 us: shards(): gathered = lax.all_gather(own_cols, 'gy', axis=0, tiled=True)]
    dot_general x3 -> x0, matrix products: 23.4 us -> none  [the longest x1 11.9 us: shards(): partial_out = jnp.dot(full_rows, w_out, preferred_element_type=jnp.float32)]
    all_to_all x1 -> x0, blocking collectives: 12 us -> none  [shards(): lax.all_to_all(attended, 'gy', split_axis=1, concat_axis=0, tiled=True)]
    all_to_all x1 -> x0, waiting for transfers between devices: 9.38 us -> none  [shards(): lax.all_to_all(packed, 'gy', split_axis=0, concat_axis=1, tiled=True)]
    all_to_all x1 -> x0, starting transfers between devices: 5.51 us -> none  [shards(): lax.all_to_all(packed, 'gy', split_axis=0, concat_axis=1, tiled=True)]
    convert_element_type x3 -> x0, other arithmetic: 4.75 us -> none  [the longest x1 2.84 us: shards(): values = hidden.astype(jnp.float32)]
  transfers between devices with their start and end apart: 5 -> 0, of which waited for: 5 -> 0; matrix products, arithmetic and copies ran while one was open for 0% -> 0% of each run, Pallas kernels for 0% -> 0%
where the time goes in v1:
time: 114 us
  Pallas kernels  103 us (90%)
  other arithmetic  4.41 us (4%)
  local copies, waits for them, and re-layouts  4.09 us (4%)
  matrix products  2.64 us (2%)
    pallas_call x1, Pallas kernels, project(): pl.pallas_call(functools.partial(project_kernel, n, chunks, tiles), out_s...  54.7 us
    pallas_call x1, Pallas kernels, combine(): pl.pallas_call(functools.partial(combine_kernel, n, chunks), out_shape=ja...  48.1 us
    unnamed x6, local copies, waits for them, and re-layouts  2.58 us

profile of v1, /device:TPU:0, one launch (start us, length us, event | category | flops | bytes accessed | tf_op | source)
XLA Modules:
  0.0 114.1 jit_solution(3491337494158399691)
XLA Ops:
  0.0 0.7 convert_element_type.35
  0.7 0.7 iota_compare_fusion
  1.4 0.1 multiply_cosine_fusion
  1.5 1.4 %reshape.105.gain_ref = bf16[1,16384]{1,0:T(2,128)(2,1)} reshape(bf16[16384]{0:T(1024)(128)(2,1)} %param.9) | data formatting | bytes 65536 | tf_op jit(solution)/shard_map/reshape | solution.py:519
  2.9 54.7 %project.1 = (bf16[8,16384]{1,0:T(8,128)(2,1)}, bf16[8,2048]{1,0:T(8,128)(2,1)}) custom-call(bf16[32,16384]{1,0:T(8,128)(2,1)} %hidden_ref.1, bf16[1,16384]{1,0:T(2,128)(2,1)} %reshape.105.gain_ref, bf16[4096,2048]{1,0:T(8,128)(2,1)} %wq_hbm.1, bf16[4096,256]{1,0:T(8,128)(2,1)} %wkv_hbm.1), custom_call_target="tpu_custom_call" | custom-call | flops 4831838208 | bytes 18874368 | tf_op jit(solution)/shard_map/project/pallas_call | solution.py:329
  57.7 0.0 copy-start
  57.7 0.9 fusion.22
  58.6 0.1 subtract_convert_fusion.1
  58.7 0.1 maximum_bitcast_fusion
  58.7 1.2 %bitcast_convert_fusion = f32[8,128,128]{2,0,1:T(8,128)S(1)} fusion(bf16[8,16384]{1,0:T(8,128)(2,1)} %get-tuple-element.7), kind=kLoop, calls=%fused_computation.17 | loop fusion | flops 131072 | bytes 786432 | tf_op jit(solution)/shard_map/reshape | solution.py:35
  59.9 0.2 subtract_convert_fusion
  60.2 0.0 copy-start.1
  60.3 0.3 fusion.19
  60.6 0.0 copy-done
  60.6 1.3 %fusion.27 = (f32[8,8,16]{2,1,0:T(8,128)S(1)}, f32[8,8,16,256]{3,2,1,0:T(8,128)S(1)}) fusion(bf16[8,256,8,128]{3,2,1,0:T(8,128)(2,1)S(1)} %copy-done, bf16[8,8,16,64]{3,2,1,0:T(8,128)(2,1)S(1)} %bitcast.29, bf16[8,8,16,64]{3,2,1,0:T(8,128)(2,1)S(1)} %bitcast.27, pred[8,256]{1,0:T(8,128)(4,1)S(1)} %iota_compare_fusion), kind=kOutput, calls=%fused_computation.38 | convolution fusion | flops 68418560 | bytes 5511168 | tf_op jit(solution)/shard_map/rgqd,rtgd->rgqt/dot_general | solution.py:42
  61.9 0.4 fusion.16
  62.4 0.0 copy-done.1
  62.4 1.0 fusion.13
  63.4 0.9 copy.34
  64.3 48.1 %combine.1 = bf16[32,4096]{1,0:T(8,128)(2,1)} custom-call(bf16[8,16384]{1,0:T(8,128)(2,1)} %bitcast.25, bf16[2048,4096]{1,0:T(8,128)(2,1)} %w_hbm.1), custom_call_target="tpu_custom_call" | custom-call | flops 4294967296 | bytes 16777216 | tf_op jit(solution)/shard_map/combine/pallas_call | solution.py:485
  112.4 1.7 %copy.36 = bf16[32,4096]{1,0:T(8,128)(2,1)} copy(bf16[32,4096]{1,0:T(8,128)(2,1)} %combine.1) | data formatting | bytes 524288
  (6 shorter events, 0.1 us)
Async XLA Ops:
  57.7 2.9 %copy-start = (bf16[8,256,8,128]{3,2,1,0:T(8,128)(2,1)S(1)}, bf16[8,256,8,128]{3,2,1,0:T(8,128)(2,1)}, u32[]{:S(2)}) copy-start(bf16[8,256,8,128]{3,2,1,0:T(8,128)(2,1)} %param.12) | copy-start | bytes 12582916
  60.2 2.2 %copy-start.1 = (bf16[8,256,8,128]{3,2,1,0:T(8,128)(2,1)S(1)}, bf16[8,256,8,128]{3,2,1,0:T(8,128)(2,1)}, u32[]{:S(2)}) copy-start(bf16[8,256,8,128]{3,2,1,0:T(8,128)(2,1)} %param.13) | copy-start | bytes 12582916

commit v2 on v1

--- a/solution.py
+++ b/solution.py
@@ -10,6 +10,7 @@
 
 MESH = pl.DeviceIdType.MESH
 VMEM_BYTES = 56 * 2**20
+GROUP = 2
 
 
 def rotate_heads(values, position, head_dim):
@@ -73,7 +74,10 @@
         )
     pl.semaphore_signal(barrier, inc=1, device_id=(sibling(gx), me), device_id_type=MESH)
     pl.semaphore_signal(barrier, inc=1, device_id=(across(gx), me), device_id_type=MESH)
-    pl.semaphore_wait(barrier, n + 1)
+
+
+def met(n):
+    pl.semaphore_wait(pltpu.get_barrier_semaphore(), n + 1)
 
 
 def sibling(gx):
@@ -119,6 +123,7 @@
     width = chunks * xg.shape[2]
     piece = xg.shape[2]
     hops = n // 2
+    meet(n, gx, me)
     loads = []
     for c in range(chunks):
         loads.append(
@@ -169,11 +174,11 @@
     for c in range(chunks):
         offset = pl.multiple_of(gx * width + c * piece, piece)
         block = hidden_ref[:, pl.ds(offset, piece)].astype(jnp.float32)
-        gain = gain_ref[:, pl.ds(offset, piece)].astype(jnp.float32)
+        gain = gain_ref[pl.ds(offset, piece)].astype(jnp.float32).reshape(1, piece)
         xg[c, pl.ds(pl.multiple_of(me * rows, rows), rows), :] = (
             block * inverse * gain
         ).astype(jnp.bfloat16)
-    meet(n, gx, me)
+    met(n)
 
     started = []
 
@@ -211,40 +216,45 @@
     def part(gxi):
         return pl.ds(pl.multiple_of(gxi * part_rows, part_rows), part_rows)
 
+    def multiply(c):
+        for d in (0, 1):
+            if used(d, c, hops - 1):
+                ring_in(d, c, hops - 1).wait_recv()
+        loads[c][0].wait()
+        loads[c][1].wait()
+        for t in range(count):
+            add_product(t, c)
+            if c == chunks - 1:
+                for x in (0, 1):
+                    s1[t][x] = acc[t][part(2 * x + 1 - core), :].astype(jnp.bfloat16)
+                copy = send(s1[t], r1[t], s1_send.at[t], s1_recv.at[t], (sibling(gx), me))
+                go(copy)
+                first.append(copy)
+
     first = []
-    for time in range(chunks + hops):
-        if time == 0:
-            for c in range(min(2, chunks)):
+    groups = [range(c, min(c + GROUP, chunks)) for c in range(0, chunks, GROUP)]
+
+    def own_sends(group):
+        for c in group:
+            for d in (0, 1):
+                if used(d, c, 0):
+                    go(ring(d, c, 0))
+
+    own_sends(groups[0])
+    for g, group in enumerate(groups):
+        for s in range(1, hops):
+            if s == hops - 1 and g + 1 < len(groups):
+                own_sends(groups[g + 1])
+            for c in group:
                 for d in (0, 1):
-                    if used(d, c, 0):
-                        go(ring(d, c, 0))
-        elif time + 1 < chunks:
-            for d in (0, 1):
-                if used(d, time + 1, 0):
-                    go(ring(d, time + 1, 0))
-        for c in range(chunks):
-            s = time - c
-            if 1 <= s < hops:
-                for d in (0, 1):
-                    if used(d, c, s - 1):
-                        ring_in(d, c, s - 1).wait_recv()
+                    ring_in(d, c, s - 1).wait_recv()
                     if used(d, c, s):
                         go(ring(d, c, s))
-        c = time - hops
-        if 0 <= c < chunks:
-            for d in (0, 1):
-                if used(d, c, hops - 1):
-                    ring_in(d, c, hops - 1).wait_recv()
-            loads[c][0].wait()
-            loads[c][1].wait()
-            for t in range(count):
-                add_product(t, c)
-                if c == chunks - 1:
-                    for x in (0, 1):
-                        s1[t][x] = acc[t][part(2 * x + 1 - core), :].astype(jnp.bfloat16)
-                    copy = send(s1[t], r1[t], s1_send.at[t], s1_recv.at[t], (sibling(gx), me))
-                    go(copy)
-                    first.append(copy)
+            if s == 1 and g > 0:
+                for c in groups[g - 1]:
+                    multiply(c)
+    for c in groups[-1]:
+        multiply(c)
     second = []
     for t in range(count):
         first[t].wait_recv()
@@ -293,7 +303,7 @@
     rows, features = hidden.shape
     width, q_cols = w_query.shape
     kv_cols = w_keyval.shape[1]
-    chunks = 4
+    chunks = 2
     piece = width // chunks
     total = rows * n
     step = min(1024, q_cols)
@@ -365,6 +375,9 @@
         pltpu.make_async_copy(w_hbm.at[:, pl.ds(c * piece, piece)], w.at[c], w_sem.at[c])
         for c in range(chunks)
     ]
+    meet(n, gx, me)
+    for load in loads:
+        load.start()
     for p in range(n):
         block = att_ref[:, p * columns : (p + 1) * columns].astype(jnp.float32)
         packed[p] = halves_stacked(block).astype(jnp.bfloat16)
@@ -374,12 +387,10 @@
         copy.start()
         started.append(copy)
 
-    meet(n, gx, me)
+    met(n)
     for k in range(1, n):
         to = lax.rem(me + k, n)
         go(send(packed.at[to], xa.at[gx, me], a_send.at[k], a_recv.at[k], (gx, to)))
-    for load in loads:
-        load.start()
     xa[gx, me] = packed[me]
     other = across(gx)
     twin = sibling(gx)
@@ -440,33 +451,30 @@
         go(hop(d, c, s))
 
     step = min(512, piece)
-    for time in range(chunks + hops):
+    for c in range(chunks):
+        loads[c].wait()
+
+        def body(k, carry):
+            at = pl.multiple_of(k * step, step)
+            part[c, :, pl.ds(at, step)] = jnp.dot(
+                xs[...], w[c, :, pl.ds(at, step)], preferred_element_type=jnp.float32
+            )
+            return carry
+
+        lax.fori_loop(0, piece // step, body, 0)
+        for d in (0, 1):
+            pass_on(d, c, 0 if used(d, c, 0) else 1)
+    for s in range(1, hops):
         for c in range(chunks):
-            s = time - c
-            if 1 <= s < hops:
-                for d in (0, 1):
+            for d in (0, 1):
+                if s > 1 or used(d, c, 0):
                     pass_on(d, c, s)
-            if s == hops:
-                value = own(c, me)
-                for d in (0, 1):
-                    hop(d, c, hops - 1).wait_recv()
-                    value = value + ringbuf[d, c, hops - 1].astype(jnp.float32)
-                out_ref[:, c * piece : (c + 1) * piece] = value.astype(jnp.bfloat16)
-        if time < chunks:
-            c = time
-            loads[c].wait()
-
-            def body(k, carry):
-                at = pl.multiple_of(k * step, step)
-                part[c, :, pl.ds(at, step)] = jnp.dot(
-                    xs[...], w[c, :, pl.ds(at, step)], preferred_element_type=jnp.float32
-                )
-                return carry
-
-            lax.fori_loop(0, piece // step, body, 0)
-            for d in (0, 1):
-                if used(d, c, 0):
-                    pass_on(d, c, 0)
+    for c in range(chunks):
+        value = own(c, me)
+        for d in (0, 1):
+            hop(d, c, hops - 1).wait_recv()
+            value = value + ringbuf[d, c, hops - 1].astype(jnp.float32)
+        out_ref[:, c * piece : (c + 1) * piece] = value.astype(jnp.bfloat16)
     for copy in started:
         copy.wait_send()
 
@@ -516,7 +524,7 @@
 
 def shards(hidden, norm_gain, w_query, w_keyval, key_cache, value_cache, lengths, w_out):
     peers = lax.axis_size("gy")
-    query, keyval = project(hidden, norm_gain.reshape(1, -1), w_query, w_keyval, peers)
+    query, keyval = project(hidden, norm_gain, w_query, w_keyval, peers)
     attended = attend_rows(query, keyval, key_cache, value_cache, lengths)
     return combine(attended, w_out, peers)
 

time: 114 us -> 99.4 us (0.87)
  Pallas kernels: 103 us -> 89.3 us
  local copies, waits for them, and re-layouts: 4.09 us -> 2.67 us
    pallas_call x1, Pallas kernels: 48.1 us -> 39.4 us  [combine(): pl.pallas_call(functools.partial(combine_kernel, n, chunks), out_shape=ja...]
    pallas_call x1, Pallas kernels: 54.7 us -> 49.9 us  [project(): pl.pallas_call(functools.partial(project_kernel, n, chunks, tiles), out_s...]
    reshape x1 -> x0, local copies, waits for them, and re-layouts: 1.43 us -> none  [shards(): norm_gain.reshape(1, -1)]
where the time goes in v2:
time: 99.4 us; the launch traced here: 99.2 us
  Pallas kernels  89.3 us (90%)
  other arithmetic  4.41 us (4%)
  local copies, waits for them, and re-layouts  2.67 us (3%)
  matrix products  2.64 us (3%)
    pallas_call x1, Pallas kernels, project(): pl.pallas_call(functools.partial(project_kernel, n, chunks, tiles), out_s...  49.9 us
    pallas_call x1, Pallas kernels, combine(): pl.pallas_call(functools.partial(combine_kernel, n, chunks), out_shape=ja...  39.4 us
    unnamed x6, local copies, waits for them, and re-layouts  2.58 us

profile of v2, /device:TPU:0, one launch (start us, length us, event | category | flops | bytes accessed | tf_op | source)
XLA Modules:
  0.0 99.2 jit_solution(290755242581003024)
XLA Ops:
  0.0 0.7 convert_element_type.35
  0.7 0.7 iota_compare_fusion
  1.4 0.1 multiply_cosine_fusion
  1.5 49.9 %project.1 = (bf16[8,16384]{1,0:T(8,128)(2,1)}, bf16[8,2048]{1,0:T(8,128)(2,1)}) custom-call(bf16[32,16384]{1,0:T(8,128)(2,1)} %hidden_ref.1, bf16[16384]{0:T(1024)(128)(2,1)} %gain_ref.1, bf16[4096,2048]{1,0:T(8,128)(2,1)} %wq_hbm.1, bf16[4096,256]{1,0:T(8,128)(2,1)} %wkv_hbm.1), custom_call_target="tpu_custom_call" | custom-call | flops 4831838208 | bytes 18874368 | tf_op jit(solution)/shard_map/project/pallas_call | solution.py:339
  51.4 0.0 copy-start
  51.4 0.9 fusion.22
  52.3 0.1 subtract_convert_fusion.1
  52.4 0.1 maximum_bitcast_fusion
  52.5 1.2 %bitcast_convert_fusion = f32[8,128,128]{2,0,1:T(8,128)S(1)} fusion(bf16[8,16384]{1,0:T(8,128)(2,1)} %get-tuple-element.7), kind=kLoop, calls=%fused_computation.17 | loop fusion | flops 131072 | bytes 786432 | tf_op jit(solution)/shard_map/reshape | solution.py:36
  53.7 0.2 subtract_convert_fusion
  54.0 0.0 copy-start.1
  54.0 0.3 fusion.19
  54.4 0.0 copy-done
  54.4 1.3 %fusion.27 = (f32[8,8,16]{2,1,0:T(8,128)S(1)}, f32[8,8,16,256]{3,2,1,0:T(8,128)S(1)}) fusion(bf16[8,256,8,128]{3,2,1,0:T(8,128)(2,1)S(1)} %copy-done, bf16[8,8,16,64]{3,2,1,0:T(8,128)(2,1)S(1)} %bitcast.29, bf16[8,8,16,64]{3,2,1,0:T(8,128)(2,1)S(1)} %bitcast.27, pred[8,256]{1,0:T(8,128)(4,1)S(1)} %iota_compare_fusion), kind=kOutput, calls=%fused_computation.38 | convolution fusion | flops 68418560 | bytes 5511168 | tf_op jit(solution)/shard_map/rgqd,rtgd->rgqt/dot_general | solution.py:43
  55.7 0.4 fusion.16
  56.1 0.0 copy-done.1
  56.2 1.0 %fusion.13 = bf16[8,8,16,128]{3,2,1,0:T(8,128)(2,1)S(1)} fusion(bf16[8,256,8,128]{3,2,1,0:T(8,128)(2,1)S(1)} %copy-done.1, f32[8,8,16,256]{3,2,1,0:T(8,128)S(1)} %get-tuple-element.20, f32[8,8,16]{2,1,0:T(8,128)S(1)} %get-tuple-element.12, f32[8,8,16]{2,1,0:T(8,128)S(1)} %multiply_maximum_fusion, f32[8,8,128]{2,1,0:T(8,128)S(1)} %copy.13, ...), kind=kOutput, calls=%fused_computation.7 | convolution fusion | flops 68288512 | bytes 5550080 | tf_op jit(solution)/shard_map/rgqt,rtgd->rgqd/dot_general | solution.py:55
  57.2 0.9 copy.34
  58.1 39.4 %combine.1 = bf16[32,4096]{1,0:T(8,128)(2,1)} custom-call(bf16[8,16384]{1,0:T(8,128)(2,1)} %bitcast.25, bf16[2048,4096]{1,0:T(8,128)(2,1)} %w_hbm.1), custom_call_target="tpu_custom_call" | custom-call | flops 4294967296 | bytes 16777216 | tf_op jit(solution)/shard_map/combine/pallas_call | solution.py:493
  97.5 1.7 %copy.36 = bf16[32,4096]{1,0:T(8,128)(2,1)} copy(bf16[32,4096]{1,0:T(8,128)(2,1)} %combine.1) | data formatting | bytes 524288
  (6 shorter events, 0.1 us)
Async XLA Ops:
  51.4 2.9 %copy-start = (bf16[8,256,8,128]{3,2,1,0:T(8,128)(2,1)S(1)}, bf16[8,256,8,128]{3,2,1,0:T(8,128)(2,1)}, u32[]{:S(2)}) copy-start(bf16[8,256,8,128]{3,2,1,0:T(8,128)(2,1)} %param.12) | copy-start | bytes 12582916
  54.0 2.2 %copy-start.1 = (bf16[8,256,8,128]{3,2,1,0:T(8,128)(2,1)S(1)}, bf16[8,256,8,128]{3,2,1,0:T(8,128)(2,1)}, u32[]{:S(2)}) copy-start(bf16[8,256,8,128]{3,2,1,0:T(8,128)(2,1)} %param.13) | copy-start | bytes 12582916

commit v3 on v2

--- a/solution.py
+++ b/solution.py
@@ -155,20 +155,20 @@
     behind = index_at(place - 1, n)
     targets = (ahead, behind)
 
-    def slot(owner, c):
-        return xg.at[c, pl.ds(pl.multiple_of(owner * rows, rows), rows), :]
-
-    def used(d, c, s):
-        return s < hops - 1 or c % 2 == d
+    def slot(owner, c, d, s):
+        if s < hops - 1:
+            return xg.at[c, pl.ds(pl.multiple_of(owner * rows, rows), rows), :]
+        half = rows // 2
+        return xg.at[c, pl.ds(pl.multiple_of(owner * rows + d * half, half), half), :]
 
     def ring(d, c, s):
         owner = index_at(place - s if d == 0 else place + s, n)
-        ref = slot(owner, c)
+        ref = slot(owner, c, d, s)
         return send(ref, ref, ag_send.at[d, c, s], ag_recv.at[d, c, s], (gx, targets[d]))
 
     def ring_in(d, c, s):
         owner = index_at(place - s - 1 if d == 0 else place + s + 1, n)
-        ref = slot(owner, c)
+        ref = slot(owner, c, d, s)
         return send(ref, ref, ag_send.at[d, c, s], ag_recv.at[d, c, s], (gx, targets[d]))
 
     for c in range(chunks):
@@ -218,8 +218,7 @@
 
     def multiply(c):
         for d in (0, 1):
-            if used(d, c, hops - 1):
-                ring_in(d, c, hops - 1).wait_recv()
+            ring_in(d, c, hops - 1).wait_recv()
         loads[c][0].wait()
         loads[c][1].wait()
         for t in range(count):
@@ -237,8 +236,7 @@
     def own_sends(group):
         for c in group:
             for d in (0, 1):
-                if used(d, c, 0):
-                    go(ring(d, c, 0))
+                go(ring(d, c, 0))
 
     own_sends(groups[0])
     for g, group in enumerate(groups):
@@ -248,8 +246,7 @@
             for c in group:
                 for d in (0, 1):
                     ring_in(d, c, s - 1).wait_recv()
-                    if used(d, c, s):
-                        go(ring(d, c, s))
+                    go(ring(d, c, s))
             if s == 1 and g > 0:
                 for c in groups[g - 1]:
                     multiply(c)
@@ -306,7 +303,7 @@
     chunks = 2
     piece = width // chunks
     total = rows * n
-    step = min(1024, q_cols)
+    step = min(512, q_cols)
     tiles = [(0, k, step) for k in range(0, q_cols, step)] + [(1, 0, kv_cols)]
     count = len(tiles)
     hops = n // 2

time: 99.4 us -> 96.3 us (0.969)
  Pallas kernels: 89.3 us -> 86.2 us
    pallas_call x1, Pallas kernels: 49.9 us -> 46.9 us  [project(): pl.pallas_call(functools.partial(project_kernel, n, chunks, tiles), out_s...]
where the time goes in v3:
time: 96.3 us; the launch traced here: 96 us
  Pallas kernels  86.2 us (90%)
  other arithmetic  4.41 us (5%)
  local copies, waits for them, and re-layouts  2.67 us (3%)
  matrix products  2.64 us (3%)
    pallas_call x1, Pallas kernels, project(): pl.pallas_call(functools.partial(project_kernel, n, chunks, tiles), out_s...  46.9 us
    pallas_call x1, Pallas kernels, combine(): pl.pallas_call(functools.partial(combine_kernel, n, chunks), out_shape=ja...  39.3 us
    unnamed x6, local copies, waits for them, and re-layouts  2.58 us

profile of v3, /device:TPU:0, one launch (start us, length us, event | category | flops | bytes accessed | tf_op | source)
XLA Modules:
  0.0 96.0 jit_solution(13446148262806269072)
XLA Ops:
  0.0 0.7 convert_element_type.35
  0.7 0.7 iota_compare_fusion
  1.4 0.1 multiply_cosine_fusion
  1.5 46.9 %project.1 = (bf16[8,16384]{1,0:T(8,128)(2,1)}, bf16[8,2048]{1,0:T(8,128)(2,1)}) custom-call(bf16[32,16384]{1,0:T(8,128)(2,1)} %hidden_ref.1, bf16[16384]{0:T(1024)(128)(2,1)} %gain_ref.1, bf16[4096,2048]{1,0:T(8,128)(2,1)} %wq_hbm.1, bf16[4096,256]{1,0:T(8,128)(2,1)} %wkv_hbm.1), custom_call_target="tpu_custom_call" | custom-call | flops 4831838208 | bytes 18874368 | tf_op jit(solution)/shard_map/project/pallas_call | solution.py:336
  48.4 0.0 copy-start
  48.4 0.9 fusion.22
  49.3 0.1 subtract_convert_fusion.1
  49.4 0.1 maximum_bitcast_fusion
  49.5 1.2 %bitcast_convert_fusion = f32[8,128,128]{2,0,1:T(8,128)S(1)} fusion(bf16[8,16384]{1,0:T(8,128)(2,1)} %get-tuple-element.7), kind=kLoop, calls=%fused_computation.17 | loop fusion | flops 131072 | bytes 786432 | tf_op jit(solution)/shard_map/reshape | solution.py:36
  50.7 0.2 subtract_convert_fusion
  51.0 0.0 copy-start.1
  51.0 0.3 fusion.19
  51.3 0.0 copy-done
  51.3 1.3 %fusion.27 = (f32[8,8,16]{2,1,0:T(8,128)S(1)}, f32[8,8,16,256]{3,2,1,0:T(8,128)S(1)}) fusion(bf16[8,256,8,128]{3,2,1,0:T(8,128)(2,1)S(1)} %copy-done, bf16[8,8,16,64]{3,2,1,0:T(8,128)(2,1)S(1)} %bitcast.29, bf16[8,8,16,64]{3,2,1,0:T(8,128)(2,1)S(1)} %bitcast.27, pred[8,256]{1,0:T(8,128)(4,1)S(1)} %iota_compare_fusion), kind=kOutput, calls=%fused_computation.38 | convolution fusion | flops 68418560 | bytes 5511168 | tf_op jit(solution)/shard_map/rgqd,rtgd->rgqt/dot_general | solution.py:43
  52.7 0.4 fusion.16
  53.1 0.0 copy-done.1
  53.1 1.0 %fusion.13 = bf16[8,8,16,128]{3,2,1,0:T(8,128)(2,1)S(1)} fusion(bf16[8,256,8,128]{3,2,1,0:T(8,128)(2,1)S(1)} %copy-done.1, f32[8,8,16,256]{3,2,1,0:T(8,128)S(1)} %get-tuple-element.20, f32[8,8,16]{2,1,0:T(8,128)S(1)} %get-tuple-element.12, f32[8,8,16]{2,1,0:T(8,128)S(1)} %multiply_maximum_fusion, f32[8,8,128]{2,1,0:T(8,128)S(1)} %copy.13, ...), kind=kOutput, calls=%fused_computation.7 | convolution fusion | flops 68288512 | bytes 5550080 | tf_op jit(solution)/shard_map/rgqt,rtgd->rgqd/dot_general | solution.py:55
  54.2 0.9 copy.34
  55.0 39.3 %combine.1 = bf16[32,4096]{1,0:T(8,128)(2,1)} custom-call(bf16[8,16384]{1,0:T(8,128)(2,1)} %bitcast.25, bf16[2048,4096]{1,0:T(8,128)(2,1)} %w_hbm.1), custom_call_target="tpu_custom_call" | custom-call | flops 4294967296 | bytes 16777216 | tf_op jit(solution)/shard_map/combine/pallas_call | solution.py:490
  94.4 1.7 %copy.36 = bf16[32,4096]{1,0:T(8,128)(2,1)} copy(bf16[32,4096]{1,0:T(8,128)(2,1)} %combine.1) | data formatting | bytes 524288
  (6 shorter events, 0.1 us)
Async XLA Ops:
  48.4 2.9 %copy-start = (bf16[8,256,8,128]{3,2,1,0:T(8,128)(2,1)S(1)}, bf16[8,256,8,128]{3,2,1,0:T(8,128)(2,1)}, u32[]{:S(2)}) copy-start(bf16[8,256,8,128]{3,2,1,0:T(8,128)(2,1)} %param.12) | copy-start | bytes 12582916
  51.0 2.2 %copy-start.1 = (bf16[8,256,8,128]{3,2,1,0:T(8,128)(2,1)S(1)}, bf16[8,256,8,128]{3,2,1,0:T(8,128)(2,1)}, u32[]{:S(2)}) copy-start(bf16[8,256,8,128]{3,2,1,0:T(8,128)(2,1)} %param.13) | copy-start | bytes 12582916
